TPU v7x, 32 devices: a whole 2x2x4 slice. The times are simulated.
32 devices in a mesh: gx: 4 (over z), gy: 4 (over x, core), sa: 2 (over y).
Axes of the slice: x: 2, y: 2, z: 4, core: 2. Of those that a mesh axis runs over, the one named last changes fastest.
Arguments:
- right_side: float32 [64, 256, 256], P('gx', 'gy', 'sa'), may hold values from -8 to 8
- diagonal: float32 [64, 256, 256], P('gx', 'gy', 'sa'), may hold values from 0.25 to 2
Outputs:
- pressure: float32 [64, 256, 256], P('gx', 'gy', 'sa')
- residual: float32 [64, 256, 256], P('gx', 'gy', 'sa')
All inputs are finite; a program needn't handle non-finite values.
Results may differ from a plain program's by a relative error of at most 0.0001.
Values sent between devices are 32-bit elements; how exact they have to be, the bound alone decides.
A program may use at most 192 MiB of HBM per device.

v0:
```python
import functools

import jax
import jax.numpy as jnp
from jax import lax
from jax.experimental import pallas as pl
from jax.experimental.pallas import tpu as pltpu
from jax.sharding import PartitionSpec as P

CYCLES = 2
SWEEPS = 5
COARSE_SWEEPS = 6
W = 2.0 / 3.0
AXES = ("gx", "gy", "sa")
MESH = pl.DeviceIdType.MESH
S = 8
L = 128
UNIT = 16


class Level:
    def __init__(self, nx, nj, dz, refs):
        self.nx, self.nj, self.dz = nx, nj, dz
        self.unit = UNIT // dz
        self.sent = [False, False]
        self.E, self.F, self.G, self.YS, self.YR, self.ZS, self.ZR, self.ssem, self.rsem = refs


def scratch_of(nx, nj):
    return [
        pltpu.VMEM((2, nx + 2, nj, S, L), jnp.float32),
        pltpu.VMEM((nx, nj, S, L), jnp.float32),
        pltpu.VMEM((nx, nj, S, L), jnp.float32),
        pltpu.VMEM((2, 2, nx, L), jnp.float32),
        pltpu.VMEM((2, 2, nx, L), jnp.float32),
        pltpu.VMEM((2, S, L), jnp.float32),
        pltpu.VMEM((2, S, L), jnp.float32),
        pltpu.SemaphoreType.DMA((2, 5)),
        pltpu.SemaphoreType.DMA((2, 5)),
    ]


def kernel(sizes, nx, nj, f_hbm, d_hbm, p_ref, r_ref, *scratch):
    fine = Level(nx, nj, 1, scratch[0:9])
    coarse = Level(nx // 2, nj // 2, 2, scratch[9:18])
    PB, f_ref, d_ref, isem = scratch[18:]
    loads = [
        pltpu.make_async_copy(f_hbm, f_ref, isem.at[0]),
        pltpu.make_async_copy(d_hbm, d_ref, isem.at[1]),
    ]
    for load in loads:
        load.start()
    gx, gy, sa = (lax.axis_index(a) for a in AXES)
    ngx, ngy, _ = sizes
    has = [gx > 0, gx < ngx - 1, gy > 0, gy < ngy - 1, None]
    to = [
        (gx - 1, gy, sa),
        (gx + 1, gy, sa),
        (gx, gy - 1, sa),
        (gx, gy + 1, sa),
        (gx, gy, 1 - sa),
    ]

    lane = lax.broadcasted_iota(jnp.int32, (S, L), 1)
    row = lax.broadcasted_iota(jnp.int32, (S, L), 0)
    even = lane % 2 == 0
    zero = jnp.zeros((S, L), jnp.float32)

    def when(cond, fn):
        if cond is None:
            fn()
        else:
            pl.when(cond)(fn)

    def copies(lv, slot):
        pairs = [
            (lv.E.at[slot, 1], lv.E.at[slot, lv.nx + 1]),
            (lv.E.at[slot, lv.nx], lv.E.at[slot, 0]),
            (lv.YS.at[slot, 0], lv.YR.at[slot, 1]),
            (lv.YS.at[slot, 1], lv.YR.at[slot, 0]),
            (lv.ZS.at[slot], lv.ZR.at[slot]),
        ]
        back = [1, 0, 3, 2, 4]
        return [
            pltpu.make_async_remote_copy(
                src_ref=a,
                dst_ref=b,
                send_sem=lv.ssem.at[slot, i],
                recv_sem=lv.rsem.at[slot, back[i]],
                device_id=to[i],
                device_id_type=MESH,
            )
            for i, (a, b) in enumerate(pairs)
        ]

    def arrivals(lv, slot):
        cs = copies(lv, slot)
        return [cs[1], cs[0], cs[3], cs[2], cs[4]]

    def send(lv, slot, dirs=(2, 3, 4)):
        cs = copies(lv, slot)
        for i in dirs:
            when(has[i], cs[i].start)
        lv.sent[slot] = True

    def free(lv, slot):
        if lv.sent[slot]:
            cs = copies(lv, slot)
            for i in range(5):
                when(has[i], cs[i].wait_send)
            lv.sent[slot] = False

    def wait(lv, slot):
        ar = arrivals(lv, slot)
        for i in range(5):
            when(has[i], ar[i].wait_recv)
        free(lv, 1 - slot)

    def face(lv):
        base = jnp.where(sa == 0, L - lv.dz, 0)
        return lax.rem(lane - base + L, L) // lv.dz

    def loop(count, unit, fn, carry, early=None):
        unit = min(unit, count)

        def group(g, carry):
            for i in range(unit):
                carry = fn(g * unit, i, carry)
            return carry

        if unit == count:
            for n, i in enumerate([0, count - 1, *range(1, count - 1)]):
                carry = fn(0, i, carry)
                if n == 1 and early is not None:
                    early()
            return carry
        assert early is None
        return lax.fori_loop(0, count // unit, group, carry)

    def turn(t, by):
        by %= L
        return t if by == 0 else pltpu.roll(t, by, 1)

    def put(lv, slot, x, i, tiles, acc):
        rel = face(lv)
        for j, t in enumerate(tiles):
            lv.E[slot, x + 1, j] = t
            k = i * lv.nj + j
            acc = jnp.where(rel == k, turn(t, lv.dz * k), acc)
        lv.YS[slot, 0, pl.ds(x, 1), :] = tiles[0][0:1]
        lv.YS[slot, 1, pl.ds(x, 1), :] = tiles[-1][S - 1 : S]
        return turn(acc, -lv.dz * lv.nj * lv.unit) if i == lv.unit - 1 < lv.nx - 1 else acc

    def put_end(lv, slot, acc):
        lv.ZS[slot] = turn(acc, lv.nx * lv.nj * lv.dz if lv.unit < lv.nx else 0)

    def face_start(lv, slot):
        z = lv.ZR[slot]
        return jnp.where(sa == 0, pltpu.roll(z, L - lv.dz, 1), pltpu.roll(z, lv.dz, 1))

    def around(lv, slot, x, i, halo):
        nj, dz = lv.nj, lv.dz
        mine = face(lv) == 0
        c = [lv.E[slot, x + 1, j] for j in range(nj)]
        below = jnp.where(row == 0, lv.YR[slot, 0, pl.ds(x, 1), :], pltpu.roll(c[-1], 1, 0))
        above = jnp.where(row == S - 1, lv.YR[slot, 1, pl.ds(x, 1), :], pltpu.roll(c[0], S - 1, 0))
        ext = [below] + c + [above]
        sums = []
        for j in range(nj):
            t = lv.E[slot, x, j] + lv.E[slot, x + 2, j] + (ext[j] + ext[j + 2])
            zl = jnp.where(lane < dz, 0.0, pltpu.roll(c[j], dz, 1))
            zr = jnp.where(lane >= L - dz, 0.0, pltpu.roll(c[j], L - dz, 1))
            h = turn(halo, -dz * (i * nj + j))
            sums.append(t + (zl + zr) + jnp.where(mine, h, 0.0))
        if i == lv.unit - 1 < lv.nx - 1:
            halo = turn(halo, -dz * nj * lv.unit)
        return c, sums, halo

    def sweep(lv, src, last):
        dst = 1 - src

        def plane(first, i, carry):
            halo, acc = carry
            x = first + i
            c, sums, halo = around(lv, src, x, i, halo)
            new = [
                (1.0 - W) * c[j] + lv.G[x, j] * (lv.F[x, j] + sums[j]) for j in range(lv.nj)
            ]
            if last:
                for j in range(lv.nj):
                    lv.E[dst, x + 1, j] = new[j]
            else:
                acc = put(lv, dst, x, i, new, acc)
            return halo, acc

        early = None if last else lambda: send(lv, dst, (0, 1))
        _, acc = loop(lv.nx, lv.unit, plane, (face_start(lv, src), zero), early)
        if not last:
            put_end(lv, dst, acc)

    def restrict(tiles):
        t = (tiles[0] + tiles[1]) + (tiles[2] + tiles[3])
        return 0.5 * (t + jnp.where(even, pltpu.roll(t, L - 1, 1), pltpu.roll(t, 1, 1)))

    def begin(slot, first):
        def low(start, I, acc):
            X = start + I
            new = []
            for J in range(nj // 2):
                cells = [(2 * X + i, 2 * J + k) for i in range(2) for k in range(2)]
                if first:
                    at = [(x, pl.ds(j, S, stride=nj)) for x, j in cells]
                    cf = restrict([f_ref[x, y, :] for x, y in at])
                    cd = restrict([d_ref[x, y, :] for x, y in at])
                    coarse.G[X, J] = W / (6.0 + cd)
                else:
                    cf = restrict([fine.F[x, j] for x, j in cells])
                coarse.F[X, J] = cf
                new.append(coarse.G[X, J] * cf)
            return put(coarse, slot, X, I, new, acc)

        put_end(coarse, slot, loop(nx // 2, coarse.unit, low, zero))
        if first:
            pl.semaphore_wait(barrier, count)
        send(coarse, slot, range(5))

        def high(start, i, acc):
            x = start + i
            new = []
            for j in range(nj):
                if first:
                    y = pl.ds(j, S, stride=nj)
                    f = f_ref[x, y, :]
                    g = W / (6.0 + d_ref[x, y, :])
                    fine.F[x, j] = f
                    fine.G[x, j] = g
                else:
                    f = fine.F[x, j]
                    g = fine.G[x, j]
                new.append(g * f)
            return put(fine, slot, x, i, new, acc)

        put_end(fine, slot, loop(nx, fine.unit, high, zero))
        send(fine, slot, range(5))

    for lv in (fine, coarse):
        for slot in range(2):
            for plane in (0, lv.nx + 1):
                lv.E[slot, plane] = jnp.zeros((lv.nj, S, L), jnp.float32)
            lv.YR[slot] = jnp.zeros((2, lv.nx, L), jnp.float32)

    barrier = pltpu.get_barrier_semaphore()
    for i in range(5):
        def hello(i=i):
            pl.semaphore_signal(barrier, inc=1, device_id=to[i], device_id_type=MESH)

        when(has[i], hello)
    count = 1 + sum(h.astype(jnp.int32) for h in has[:4])
    for load in loads:
        load.wait()

    slot = 0
    for cycle in range(CYCLES):
        begin(slot, cycle == 0)
        fs = cs = slot
        for step in range(max(SWEEPS, COARSE_SWEEPS) - 1):
            if step < COARSE_SWEEPS - 1:
                last = step == COARSE_SWEEPS - 2
                wait(coarse, cs)
                sweep(coarse, cs, last)
                cs = 1 - cs
                if not last:
                    send(coarse, cs)
            if step < SWEEPS - 1:
                last = step == SWEEPS - 2
                wait(fine, fs)
                sweep(fine, fs, last)
                fs = 1 - fs
                if not last:
                    send(fine, fs)

        def add(start, I, acc):
            X = start + I
            for i in range(2):
                x = 2 * X + i
                tiles = []
                for j in range(nj):
                    t = fine.E[fs, x + 1, j] + coarse.E[cs, X + 1, j // 2]
                    if cycle > 0:
                        t = t + PB[x, j]
                    if cycle < CYCLES - 1:
                        PB[x, j] = t
                    else:
                        p_ref[x, pl.ds(j, S, stride=nj), :] = t
                    tiles.append(t)
                acc = put(fine, fs, x, 2 * I + i, tiles, acc)
            return acc

        put_end(fine, fs, loop(nx // 2, coarse.unit, add, zero, lambda: send(fine, fs, (0, 1))))
        send(fine, fs)
        wait(fine, fs)

        def rest(first, i, halo):
            x = first + i
            c, sums, halo = around(fine, fs, x, i, halo)
            for j in range(nj):
                at = pl.ds(j, S, stride=nj)
                r = f_ref[x, at, :] - ((6.0 + d_ref[x, at, :]) * c[j] - sums[j])
                if cycle < CYCLES - 1:
                    fine.F[x, j] = r
                else:
                    r_ref[x, at, :] = r
            return halo

        loop(nx, fine.unit, rest, face_start(fine, fs))
        slot = 1 - fs
        free(fine, slot)
        free(coarse, slot)
    for lv in (fine, coarse):
        for at in range(2):
            free(lv, at)


def solution(mesh):
    sizes = tuple(mesh.shape[a] for a in AXES)
    assert sizes[2] == 2

    def body(right_side, diagonal):
        nx, ny, nz = right_side.shape
        assert nz == L and ny % (2 * S) == 0 and nx % 2 == 0
        nj = ny // S
        assert nx * nj <= L
        shape = jax.ShapeDtypeStruct(right_side.shape, jnp.float32)
        vmem = pl.BlockSpec(memory_space=pltpu.VMEM)
        hbm = pl.BlockSpec(memory_space=pltpu.HBM)
        return pl.pallas_call(
            functools.partial(kernel, sizes, nx, nj),
            out_shape=(shape, shape),
            in_specs=[hbm, hbm],
            out_specs=(vmem, vmem),
            scratch_shapes=scratch_of(nx, nj)
            + scratch_of(nx // 2, nj // 2)
            + [
                pltpu.VMEM((nx, nj, S, L), jnp.float32),
                pltpu.VMEM(right_side.shape, jnp.float32),
                pltpu.VMEM(right_side.shape, jnp.float32),
                pltpu.SemaphoreType.DMA((2,)),
            ],
            compiler_params=pltpu.CompilerParams(
                collective_id=0, has_side_effects=True, vmem_limit_bytes=32 * 1024 * 1024
            ),
        )(right_side, diagonal)

    return jax.shard_map(
        body,
        mesh=mesh,
        in_specs=(P(*AXES), P(*AXES)),
        out_specs=(P(*AXES), P(*AXES)),
        check_vma=False,
    )
```

profile of v0, /device:TPU:0, one launch (start us, length us, event | category | flops | bytes accessed | tf_op | source)
XLA Modules:
  0.0 46.9 jit_solution(12697754773323490362)
XLA Ops:
  0.6 0.0 copy-start
  0.6 1.0 %copy-done = f32[16,64,128]{2,1,0:T(8,128)S(1)} copy-done((f32[16,64,128]{2,1,0:T(8,128)S(1)}, f32[16,64,128]{2,1,0:T(8,128)}, u32[]{:S(2)}) %copy-start) | copy-done | bytes 524312
  1.7 0.0 copy-start.1
  1.7 1.0 %copy-done.1 = f32[16,64,128]{2,1,0:T(8,128)S(1)} copy-done((f32[16,64,128]{2,1,0:T(8,128)S(1)}, f32[16,64,128]{2,1,0:T(8,128)}, u32[]{:S(2)}) %copy-start.1) | copy-done | bytes 524312
  2.7 42.6 %shard_map.41 = (f32[16,64,128]{2,1,0:T(8,128)S(1)}, f32[16,64,128]{2,1,0:T(8,128)S(1)}) custom-call(f32[16,64,128]{2,1,0:T(8,128)S(1)} %copy-done, f32[16,64,128]{2,1,0:T(8,128)S(1)} %copy-done.1), custom_call_target="tpu_custom_call" | custom-call | tf_op jit(solution)/shard_map/pallas_call | solution.py:336
  45.3 0.8 %copy.6 = f32[16,64,128]{2,1,0:T(8,128)} copy(f32[16,64,128]{2,1,0:T(8,128)S(1)} %get-tuple-element.4) | data formatting | bytes 1048576
  46.1 0.8 %copy.7 = f32[16,64,128]{2,1,0:T(8,128)} copy(f32[16,64,128]{2,1,0:T(8,128)S(1)} %get-tuple-element.5) | data formatting | bytes 1048576
Async XLA Ops:
  0.6 1.0 %copy-start = (f32[16,64,128]{2,1,0:T(8,128)S(1)}, f32[16,64,128]{2,1,0:T(8,128)}, u32[]{:S(2)}) copy-start(f32[16,64,128]{2,1,0:T(8,128)} %f_hbm.1) | copy-start | bytes 1572868
  1.7 1.0 %copy-start.1 = (f32[16,64,128]{2,1,0:T(8,128)S(1)}, f32[16,64,128]{2,1,0:T(8,128)}, u32[]{:S(2)}) copy-start(f32[16,64,128]{2,1,0:T(8,128)} %d_hbm.1) | copy-start | bytes 1572868
where the time goes:
time: 47.1 us; the launch traced here: 46.9 us
  Pallas kernels  42.6 us (90%)
  local copies, waits for them, and re-layouts  3.66 us (8%)
  between operations  0.65 us (1%)
    pallas_call x1, Pallas kernels, body(): pl.pallas_call(functools.partial(kernel, sizes, nx, nj), out_shape=(shape...  42.6 us
    unnamed x6, local copies, waits for them, and re-layouts  3.66 us

commit v1 on v0

v1 whole, which is shorter than its diff:
```python
import functools

import jax
import jax.numpy as jnp
from jax import lax
from jax.experimental import pallas as pl
from jax.experimental.pallas import tpu as pltpu
from jax.sharding import PartitionSpec as P

CYCLES = 2
SWEEPS = 5
COARSE_SWEEPS = 6
STAGES = 3
W = 2.0 / 3.0
AXES = ("gx", "gy", "sa")
MESH = pl.DeviceIdType.MESH
S = 8
L = 128
COPIES = 32
F32 = jnp.float32
assert SWEEPS == 5 and COARSE_SWEEPS == 6


class Level:
    def __init__(self, at, nx, nj, dz, y0, refs):
        self.at, self.nx, self.nj, self.dz, self.y0 = at, nx, nj, dz, y0
        self.E, self.F, self.G, self.YC, self.ZC = refs


def level_scratch(nx, nj):
    return [
        pltpu.VMEM((3, nx + 4, nj, S, L), F32),
        pltpu.VMEM((CYCLES, nx + 2, nj, S, L), F32),
        pltpu.VMEM((nx + 2, nj, S, L), F32),
        pltpu.VMEM((2, nx, L), F32),
        pltpu.VMEM((S, L), F32),
    ]


def shared_scratch(rows):
    return [
        pltpu.VMEM((2, 2, 2, rows, L), F32),
        pltpu.VMEM((2, 2, 2, rows, L), F32),
        pltpu.VMEM((2, 4, S, L), F32),
        pltpu.VMEM((2, 4, S, L), F32),
        pltpu.VMEM((2, 2, 2, S, L), F32),
        pltpu.VMEM((2, 2, 2, S, L), F32),
        pltpu.VMEM((2, 2, 2, S, L), F32),
        pltpu.VMEM((2, 2, 2, S, L), F32),
        pltpu.VMEM((2, 2, rows, L), F32),
        pltpu.VMEM((CYCLES + 1, 2, rows, L), F32),
        pltpu.VMEM((CYCLES + 1, 2, rows, L), F32),
        pltpu.VMEM((CYCLES + 1, 2, S, L), F32),
        pltpu.VMEM((CYCLES + 1, 2, S, L), F32),
        pltpu.VMEM((2, 2, 2, S, L), F32),
    ]


def kernel(sizes, nx, nj, f_hbm, d_hbm, p_ref, r_ref, *scratch):
    fine = Level(0, nx, nj, 1, 0, scratch[0:5])
    coarse = Level(1, nx // 2, nj // 2, 2, nx, scratch[5:10])
    levels = (coarse, fine)
    YS, YR, ZS, ZR, CS, CR, ZXR, ZYR, YZR, FYS, FYR, FZS, FZR, ZXS = scratch[10:24]
    PB, PX, PY, PZ, YX, f_ref, d_ref, isem, ssem, rsem = scratch[24:]
    loads = [
        pltpu.make_async_copy(f_hbm, f_ref, isem.at[0]),
        pltpu.make_async_copy(d_hbm, d_ref, isem.at[1]),
    ]
    for load in loads:
        load.start()
    gx, gy, sa = (lax.axis_index(a) for a in AXES)
    ngx, ngy, _ = sizes
    left = sa == 0

    lane = lax.broadcasted_iota(jnp.int32, (S, L), 1)
    row = lax.broadcasted_iota(jnp.int32, (S, L), 0)
    even = lane & 1 == 0
    zero = jnp.zeros((S, L), F32)

    def present(d):
        dx, dy, _ = d
        tests = []
        if dx:
            tests.append(gx > 0 if dx < 0 else gx < ngx - 1)
        if dy:
            tests.append(gy > 0 if dy < 0 else gy < ngy - 1)
        if not tests:
            return None
        return functools.reduce(jnp.logical_and, tests)

    def device(d):
        return (gx + d[0], gy + d[1], 1 - sa if d[2] else sa)

    def when(cond, fn):
        if cond is None:
            fn()
        else:
            pl.when(cond)(fn)

    near = [(x, y, z) for x in (-1, 0, 1) for y in (-1, 0, 1) for z in (0, 1) if abs(x) + abs(y) + z in (1, 2)]

    def entries(rnd):
        cycle, stage = divmod(rnd, STAGES)
        q = rnd % 2
        out = []
        for u, dx in enumerate((-1, 1)):
            out.append(("edges", ZXS.at[q, u], ZXR.at[q, 1 - u], (dx, 0, 1)))
            for v, dy in enumerate((-1, 1)):
                out.append(("edges", CS.at[q, u, v], CR.at[q, 1 - u, 1 - v], (dx, dy, 0)))
        for lv in levels:
            n = lv.nx
            k = 1 if lv is fine and stage == STAGES - 1 else 2
            low, high = (2, k), (2 + n - k, k)
            to_low, to_high = (2 - k, k), (2 + n, k)
            if stage == 0:
                for ref in [lv.F.at[cycle]] + [lv.G] * (cycle == 0):
                    out.append(("planes", ref.at[1], ref.at[1 + n], (-1, 0, 0)))
                    out.append(("planes", ref.at[n], ref.at[0], (1, 0, 0)))
                low, high, to_low, to_high = (3, 1), (n, 1), (0, 1), (3 + n, 1)
            out.append(("planes", lv.E.at[q, pl.ds(*low)], lv.E.at[q, pl.ds(*to_high)], (-1, 0, 0)))
            out.append(("planes", lv.E.at[q, pl.ds(*high)], lv.E.at[q, pl.ds(*to_low)], (1, 0, 0)))
        out.append(("small", ZS.at[q], ZR.at[q], (0, 0, 1)))
        for v, dy in enumerate((-1, 1)):
            out.append(("small", YS.at[q, v, 0], YZR.at[q, 1 - v], (0, dy, 1)))
            out.append(("small", ZS.at[q, pl.ds(0, 2)], ZYR.at[q, 1 - v], (0, dy, 1)))
            out.append(("small", YS.at[q, v], YR.at[q, 1 - v], (0, dy, 0)))
        if stage == 0:
            for i in [cycle] + [CYCLES] * (cycle == 0):
                out.append(("small", FZS.at[i], FZR.at[i], (0, 0, 1)))
                for v, dy in enumerate((-1, 1)):
                    out.append(("small", FYS.at[i, v], FYR.at[i, 1 - v], (0, dy, 0)))
        assert len(out) <= COPIES
        return list(enumerate(out))

    def copy_of(rnd, i, entry):
        _, src, dst, d = entry
        return pltpu.make_async_remote_copy(
            src_ref=src,
            dst_ref=dst,
            send_sem=ssem.at[rnd, i],
            recv_sem=rsem.at[rnd, i],
            device_id=device(d),
            device_id_type=MESH,
        )

    def each(rnd, kinds, fn, sign=1):
        groups = {}
        for i, e in entries(rnd):
            if e[0] in kinds:
                groups.setdefault(e[3], []).append((i, e))
        for (dx, dy, dz), group in groups.items():

            def some(group=group):
                for i, e in group:
                    fn(copy_of(rnd, i, e))

            when(present((sign * dx, sign * dy, dz)), some)

    def send(rnd, *kinds):
        each(rnd, kinds, lambda c: c.start())

    def wait(rnd, *kinds):
        each(rnd, kinds, lambda c: c.wait_recv(), -1)

    def drain(rnd):
        each(rnd, ("edges", "planes", "small"), lambda c: c.wait_send())

    def turn(t, by):
        by %= L
        return t if by == 0 else pltpu.roll(t, by, 1)

    def from_edge(lv, depth):
        base = jnp.where(left, L - lv.dz * (depth + 1), lv.dz * depth)
        at = (lane - base) & (L - 1)
        return at if lv.dz == 1 else at >> 1

    edge = {lv: [from_edge(lv, depth) for depth in range(2)] for lv in levels}

    def pack(lv, k, t, accs):
        t = turn(t, lv.dz * k)
        return [jnp.where(edge[lv][i] == k, t, a) for i, a in enumerate(accs)]

    def packed(lv, acc, depth=0):
        return jnp.where(left, turn(acc, lv.dz * (depth + 1)), turn(acc, -lv.dz * depth))

    def put(lv, slot, q, x, tiles, accs):
        for j, t in enumerate(tiles):
            lv.E[slot, x + 2, j] = t
            accs = pack(lv, x * lv.nj + j, t, accs)
        at = slice(lv.y0 + x, lv.y0 + x + 1)
        for depth in range(2):
            YS[q, 0, depth, at, :] = tiles[depth][0:1]
            YS[q, 1, depth, at, :] = tiles[-1 - depth][S - 1 : S]
        if x in (0, lv.nx - 1):
            u = 0 if x == 0 else 1
            for v, t in enumerate((tiles[0][0:1], tiles[-1][S - 1 : S])):
                CS[q, u, v, lv.at : lv.at + 1, :] = t
            acc = zero
            for j, t in enumerate(tiles):
                (acc,) = pack(lv, j, t, [acc])
            ZXS[q, u, lv.at] = packed(lv, acc)
        return accs

    def put_end(lv, q, accs):
        for depth, acc in enumerate(accs):
            ZS[q, 2 * depth + lv.at] = packed(lv, acc, depth)

    def put_face(lv, i, x, tiles, acc):
        for j, t in enumerate(tiles):
            (acc,) = pack(lv, x * lv.nj + j, t, [acc])
        at = slice(lv.y0 + x, lv.y0 + x + 1)
        FYS[i, 0, at, :] = tiles[0][0:1]
        FYS[i, 1, at, :] = tiles[-1][S - 1 : S]
        return acc

    def outer(lv):
        return [0, 1, lv.nx - 2, lv.nx - 1]

    def inner(lv):
        return list(range(2, lv.nx - 2))

    def halo_of(lv, z):
        return jnp.where(left, turn(z, -lv.dz), z)

    def around(lv, slot, x, k, halo, rows):
        nj, dz = lv.nj, lv.dz
        mine = edge[lv][0] == 0
        c = [lv.E[slot, x + 2, j] for j in range(nj)]
        below = jnp.where(row == 0, rows[0], pltpu.roll(c[-1], 1, 0))
        above = jnp.where(row == S - 1, rows[1], pltpu.roll(c[0], S - 1, 0))
        ext = [below] + c + [above]
        sums = []
        for j in range(nj):
            t = lv.E[slot, x + 1, j] + lv.E[slot, x + 3, j] + (ext[j] + ext[j + 2])
            zl = jnp.where(lane < dz, 0.0, pltpu.roll(c[j], dz, 1))
            zr = jnp.where(lane >= L - dz, 0.0, pltpu.roll(c[j], L - dz, 1))
            h = turn(halo, -dz * (k + j))
            sums.append(t + (zl + zr) + jnp.where(mine, h, 0.0))
        return c, sums

    def step(lv, cycle, x, c, sums):
        return [
            (1.0 - W) * c[j] + lv.G[x + 1, j] * (lv.F[cycle, x + 1, j] + sums[j]) for j in range(lv.nj)
        ]

    def y_rows(lv, ref, x):
        at = lv.y0 + x
        return [ref[v, at : at + 1, :] for v in range(2)]

    def own_plane(lv, cycle, src, x, halo, rows):
        c, sums = around(lv, src, x, x * lv.nj, halo, rows)
        return step(lv, cycle, x, c, sums)

    def store(lv, slot, x, tiles):
        for j, t in enumerate(tiles):
            lv.E[slot, x + 2, j] = t

    def first_sweep(lv, cycle, q, xs):
        halo = halo_of(lv, ZR[q, lv.at])
        for x in xs:
            at = lv.y0 + x
            rows = [YR[q, v, 0, at : at + 1, :] for v in range(2)]
            store(lv, 2, x, own_plane(lv, cycle, q, x, halo, rows))

    def x_faces(lv, cycle, q):
        for u, x in enumerate((-1, lv.nx)):
            halo = halo_of(lv, ZXR[q, u, lv.at])
            rows = [CR[q, u, v, lv.at : lv.at + 1, :] for v in range(2)]
            c, sums = around(lv, q, x, 0, halo, rows)
            store(lv, 2, x, step(lv, cycle, x, c, sums))

    def y_faces(lv, cycle, q):
        tiles = lv.nx // S
        for v in range(2):
            at = [pl.ds(lv.y0 + S * t, S) for t in range(tiles)]
            c = [YR[q, v, 0, a, :] for a in at]
            for t, a in enumerate(at):
                before = CR[q, 0, v, lv.at : lv.at + 1, :] if t == 0 else pltpu.roll(c[t - 1], 1, 0)
                after = CR[q, 1, v, lv.at : lv.at + 1, :] if t == tiles - 1 else pltpu.roll(c[t + 1], S - 1, 0)
                xm = jnp.where(row == 0, before, pltpu.roll(c[t], 1, 0))
                xp = jnp.where(row == S - 1, after, pltpu.roll(c[t], S - 1, 0))
                z = YZR[q, v, a, :]
                zp = turn(jnp.where(lane < lv.dz, jnp.where(left, z, 0.0), c[t]), -lv.dz)
                zm = turn(jnp.where(lane >= L - lv.dz, jnp.where(left, 0.0, z), c[t]), lv.dz)
                sums = (xm + xp) + (YR[q, v, 1, a, :] + YS[q, v, 0, a, :]) + (zm + zp)
                g, f = FYR[CYCLES, v, a, :], FYR[cycle, v, a, :]
                lv.YC[v, pl.ds(S * t, S), :] = (1.0 - W) * c[t] + g * (f + sums)

    def z_face(lv, cycle, q):
        dz, n = lv.dz, lv.nj * lv.dz
        last = (lv.nx - 1) * n
        c = ZR[q, lv.at]
        xm = jnp.where(lane < n, ZXR[q, 0, lv.at], turn(c, n))
        xp = jnp.where(lane >= last, turn(ZXR[q, 1, lv.at], last), turn(c, -n))
        a = lane & (n - 1)
        low = turn(jnp.where(row == S - 1, ZYR[q, 0, lv.at], c), dz - n)
        high = turn(jnp.where(row == 0, ZYR[q, 1, lv.at], c), n - dz)
        ym = jnp.where(a < dz, pltpu.roll(low, 1, 0), turn(c, dz))
        yp = jnp.where(a >= n - dz, pltpu.roll(high, S - 1, 0), turn(c, -dz))
        sums = (xm + xp) + (ym + yp) + (ZR[q, 2 + lv.at] + ZS[q, lv.at])
        lv.ZC[...] = (1.0 - W) * c + FZR[CYCLES, lv.at] * (FZR[cycle, lv.at] + sums)

    def second_sweep(lv, cycle, q, xs, accs):
        halo = halo_of(lv, lv.ZC[...])
        for x in xs:
            rows = [lv.YC[v, x : x + 1, :] for v in range(2)]
            accs = put(lv, q, q, x, own_plane(lv, cycle, 2, x, halo, rows), accs)
        return accs

    def restrict(tiles):
        t = (tiles[0] + tiles[1]) + (tiles[2] + tiles[3])
        return 0.5 * (t + jnp.where(even, pltpu.roll(t, L - 1, 1), pltpu.roll(t, 1, 1)))

    def begin_coarse(cycle, q, xs, carry):
        first = cycle == 0
        accs, fz, gz = carry
        for X in xs:
            new, fs, gs = [], [], []
            for J in range(nj // 2):
                cells = [(2 * X + i, 2 * J + k) for i in range(2) for k in range(2)]
                if first:
                    at = [(x, pl.ds(j, S, stride=nj)) for x, j in cells]
                    cf = restrict([f_ref[x, y, :] for x, y in at])
                    cd = restrict([d_ref[x, y, :] for x, y in at])
                    g = W / (6.0 + cd)
                    coarse.G[X + 1, J] = g
                else:
                    cf = restrict([fine.F[cycle, x + 1, j] for x, j in cells])
                    g = coarse.G[X + 1, J]
                coarse.F[cycle, X + 1, J] = cf
                fs.append(cf)
                gs.append(g)
                new.append(g * cf)
            accs = put(coarse, q, q, X, new, accs)
            fz = put_face(coarse, cycle, X, fs, fz)
            if first:
                gz = put_face(coarse, CYCLES, X, gs, gz)
        return accs, fz, gz

    def begin_fine(cycle, q, xs, carry):
        first = cycle == 0
        accs, fz, gz = carry
        for x in xs:
            new, fs, gs = [], [], []
            for j in range(nj):
                if first:
                    y = pl.ds(j, S, stride=nj)
                    f = f_ref[x, y, :]
                    g = W / (6.0 + d_ref[x, y, :])
                    fine.F[cycle, x + 1, j] = f
                    fine.G[x + 1, j] = g
                else:
                    f = fine.F[cycle, x + 1, j]
                    g = fine.G[x + 1, j]
                fs.append(f)
                gs.append(g)
                new.append(g * f)
            accs = put(fine, q, q, x, new, accs)
            fz = put_face(fine, cycle, x, fs, fz)
            if first:
                gz = put_face(fine, CYCLES, x, gs, gz)
        return accs, fz, gz

    def begin(cycle, before=None):
        rnd = STAGES * cycle
        q = rnd % 2
        start = ([zero] * 2, zero, zero)
        if before is not None:
            before([0, 1, 2, 3, nx - 4, nx - 3, nx - 2, nx - 1])
        low = begin_coarse(cycle, q, outer(coarse), start)
        high = begin_fine(cycle, q, outer(fine), start)
        if cycle == 0:
            pl.semaphore_wait(barrier, count)
        send(rnd, "edges", "planes")
        if before is not None:
            before(range(4, nx - 4))
        low = begin_coarse(cycle, q, inner(coarse), low)
        high = begin_fine(cycle, q, inner(fine), high)
        for lv, (accs, fz, gz) in ((coarse, low), (fine, high)):
            put_end(lv, q, accs)
            FZS[cycle, lv.at] = packed(lv, fz)
            if cycle == 0:
                FZS[CYCLES, lv.at] = packed(lv, gz)
        send(rnd, "small")

    for lv in levels:
        for slot in range(2):
            for plane in (0, 1, lv.nx + 2, lv.nx + 3):
                lv.E[slot, plane] = jnp.zeros((lv.nj, S, L), F32)
        for plane in (0, lv.nx + 1):
            for cycle in range(CYCLES):
                lv.F[cycle, plane] = jnp.zeros((lv.nj, S, L), F32)
            lv.G[plane] = jnp.zeros((lv.nj, S, L), F32)
    for ref in (YR, CR, CS, ZXR, ZYR, YZR, FYR):
        ref[...] = jnp.zeros(ref.shape, F32)

    barrier = pltpu.get_barrier_semaphore()
    count = 0
    for d in near:
        cond = present(d)
        when(cond, lambda d=d: pl.semaphore_signal(barrier, inc=1, device_id=device(d), device_id_type=MESH))
        count = count + (1 if cond is None else cond.astype(jnp.int32))
    for load in loads:
        load.wait()

    begin(0)
    for cycle in range(CYCLES):
        for stage in range(STAGES):
            rnd = STAGES * cycle + stage
            q = rnd % 2
            last = stage == STAGES - 1
            swept = levels[: 1 if last else 2]
            wait(rnd, "edges", "small")
            for lv in swept:
                first_sweep(lv, cycle, q, range(1, lv.nx - 1))
                y_faces(lv, cycle, q)
                z_face(lv, cycle, q)
            wait(rnd, "planes")
            if stage == 0:
                for lv in levels:
                    for x in (-1, lv.nx):
                        for j in range(lv.nj):
                            lv.E[q, x + 2, j] = lv.G[x + 1, j] * lv.F[cycle, x + 1, j]
            for lv in swept:
                first_sweep(lv, cycle, q, (0, lv.nx - 1))
                x_faces(lv, cycle, q)
            if not last:
                accs = [second_sweep(lv, cycle, 1 - q, outer(lv), [zero] * 2) for lv in levels]
                send(rnd + 1, "edges", "planes")
                for lv, acc in zip(levels, accs):
                    put_end(lv, 1 - q, second_sweep(lv, cycle, 1 - q, inner(lv), acc))
                send(rnd + 1, "small")
                drain(rnd)

        for x in range(-1, nx + 1):
            own = 0 <= x < nx
            for j in range(nj):
                t = fine.E[q, x + 2, j] + coarse.E[2, x // 2 + 2, j // 2]
                if cycle > 0:
                    t = t + (PB[x, j] if own else PX[0 if x < 0 else 1, j])
                fine.E[2, x + 2, j] = t
                if not own:
                    PX[0 if x < 0 else 1, j] = t
                elif cycle < CYCLES - 1:
                    PB[x, j] = t
                else:
                    p_ref[x, pl.ds(j, S, stride=nj), :] = t
        for v in range(2):
            for i in range(2):
                YX[v, pl.ds(i, coarse.nx, stride=2), :] = coarse.YC[v]
            t = YR[q, v, 0, 0:nx, :] + YX[v]
            PY[v] = t if cycle == 0 else t + PY[v]
        z = coarse.ZC[...]
        t = zero
        for x in range(nx):
            here = (lane >= nj * x) & (lane < nj * (x + 1))
            t = jnp.where(here, turn(z, nj * (x - x // 2)), t)
        t = t + ZR[q, 0]
        PZ[...] = t if cycle == 0 else t + PZ[...]

        def rest(xs, cycle=cycle):
            halo = halo_of(fine, PZ[...])
            for x in xs:
                c, sums = around(fine, 2, x, x * nj, halo, [PY[v, x : x + 1, :] for v in range(2)])
                for j in range(nj):
                    at = pl.ds(j, S, stride=nj)
                    r = f_ref[x, at, :] - ((6.0 + d_ref[x, at, :]) * c[j] - sums[j])
                    if cycle < CYCLES - 1:
                        fine.F[cycle + 1, x + 1, j] = r
                    else:
                        r_ref[x, at, :] = r

        if cycle < CYCLES - 1:
            begin(cycle + 1, rest)
        else:
            rest(range(nx))
        drain(STAGES * cycle + STAGES - 1)


def solution(mesh):
    sizes = tuple(mesh.shape[a] for a in AXES)
    assert sizes[2] == 2

    def body(right_side, diagonal):
        nx, ny, nz = right_side.shape
        nj = ny // S
        assert nz == L and ny % (2 * S) == 0 and nx % (2 * S) == 0 and nx * nj == L and nj & (nj - 1) == 0
        shape = jax.ShapeDtypeStruct(right_side.shape, F32)
        vmem = pl.BlockSpec(memory_space=pltpu.VMEM)
        hbm = pl.BlockSpec(memory_space=pltpu.HBM)
        return pl.pallas_call(
            functools.partial(kernel, sizes, nx, nj),
            out_shape=(shape, shape),
            in_specs=[hbm, hbm],
            out_specs=(vmem, vmem),
            scratch_shapes=level_scratch(nx, nj)
            + level_scratch(nx // 2, nj // 2)
            + shared_scratch(nx + nx // 2)
            + [
                pltpu.VMEM((nx, nj, S, L), F32),
                pltpu.VMEM((2, nj, S, L), F32),
                pltpu.VMEM((2, nx, L), F32),
                pltpu.VMEM((S, L), F32),
                pltpu.VMEM((2, nx, L), F32),
                pltpu.VMEM(right_side.shape, F32),
                pltpu.VMEM(right_side.shape, F32),
                pltpu.SemaphoreType.DMA((2,)),
                pltpu.SemaphoreType.DMA((CYCLES * STAGES, COPIES)),
                pltpu.SemaphoreType.DMA((CYCLES * STAGES, COPIES)),
            ],
            compiler_params=pltpu.CompilerParams(
                collective_id=0, has_side_effects=True, vmem_limit_bytes=32 * 1024 * 1024
            ),
        )(right_side, diagonal)

    return jax.shard_map(
        body,
        mesh=mesh,
        in_specs=(P(*AXES), P(*AXES)),
        out_specs=(P(*AXES), P(*AXES)),
        check_vma=False,
    )
```

time: 47.1 us -> 46.5 us (0.987)
  Pallas kernels: 42.6 us -> 42 us
    pallas_call x1, Pallas kernels: 42.6 us -> 42 us  [body(): pl.pallas_call(functools.partial(kernel, sizes, nx, nj), out_shape=(shape...]
where the time goes in v1:
time: 46.5 us; the launch traced here: 46.3 us
  Pallas kernels  42 us (90%)
  local copies, waits for them, and re-layouts  3.66 us (8%)
  between operations  0.65 us (1%)
    pallas_call x1, Pallas kernels, body(): pl.pallas_call(functools.partial(kernel, sizes, nx, nj), out_shape=(shape...  42 us
    unnamed x6, local copies, waits for them, and re-layouts  3.66 us

profile of v1, /device:TPU:0, one launch (start us, length us, event | category | flops | bytes accessed | tf_op | source)
XLA Modules:
  0.0 46.3 jit_solution(1231639411653043020)
XLA Ops:
  0.6 0.0 copy-start
  0.6 1.0 %copy-done = f32[16,64,128]{2,1,0:T(8,128)S(1)} copy-done((f32[16,64,128]{2,1,0:T(8,128)S(1)}, f32[16,64,128]{2,1,0:T(8,128)}, u32[]{:S(2)}) %copy-start) | copy-done | bytes 524312
  1.7 0.0 copy-start.1
  1.7 1.0 %copy-done.1 = f32[16,64,128]{2,1,0:T(8,128)S(1)} copy-done((f32[16,64,128]{2,1,0:T(8,128)S(1)}, f32[16,64,128]{2,1,0:T(8,128)}, u32[]{:S(2)}) %copy-start.1) | copy-done | bytes 524312
  2.7 42.0 %shard_map.41 = (f32[16,64,128]{2,1,0:T(8,128)S(1)}, f32[16,64,128]{2,1,0:T(8,128)S(1)}) custom-call(f32[16,64,128]{2,1,0:T(8,128)S(1)} %copy-done, f32[16,64,128]{2,1,0:T(8,128)S(1)} %copy-done.1), custom_call_target="tpu_custom_call" | custom-call | tf_op jit(solution)/shard_map/pallas_call | solution.py:491
  44.7 0.8 %copy.6 = f32[16,64,128]{2,1,0:T(8,128)} copy(f32[16,64,128]{2,1,0:T(8,128)S(1)} %get-tuple-element.4) | data formatting | bytes 1048576
  45.5 0.8 %copy.7 = f32[16,64,128]{2,1,0:T(8,128)} copy(f32[16,64,128]{2,1,0:T(8,128)S(1)} %get-tuple-element.5) | data formatting | bytes 1048576
Async XLA Ops:
  0.6 1.0 %copy-start = (f32[16,64,128]{2,1,0:T(8,128)S(1)}, f32[16,64,128]{2,1,0:T(8,128)}, u32[]{:S(2)}) copy-start(f32[16,64,128]{2,1,0:T(8,128)} %f_hbm.1) | copy-start | bytes 1572868
  1.7 1.0 %copy-start.1 = (f32[16,64,128]{2,1,0:T(8,128)S(1)}, f32[16,64,128]{2,1,0:T(8,128)}, u32[]{:S(2)}) copy-start(f32[16,64,128]{2,1,0:T(8,128)} %d_hbm.1) | copy-start | bytes 1572868

commit v2 on v1

--- a/solution.py
+++ b/solution.py
@@ -16,28 +16,34 @@
 MESH = pl.DeviceIdType.MESH
 S = 8
 L = 128
-COPIES = 32
+COPIES = 22
 F32 = jnp.float32
 assert SWEEPS == 5 and COARSE_SWEEPS == 6
+
+
+def field_of(cycle):
+    return CYCLES - 1 - cycle
 
 
 class Level:
     def __init__(self, at, nx, nj, dz, y0, refs):
         self.at, self.nx, self.nj, self.dz, self.y0 = at, nx, nj, dz, y0
-        self.E, self.F, self.G, self.YC, self.ZC = refs
+        self.E, self.FG, self.YC, self.ZC, self.ZN = refs
+        self.F = [self.FG.at[field_of(cycle)] for cycle in range(CYCLES)]
+        self.G = self.FG.at[CYCLES]
 
 
 def level_scratch(nx, nj):
     return [
         pltpu.VMEM((3, nx + 4, nj, S, L), F32),
-        pltpu.VMEM((CYCLES, nx + 2, nj, S, L), F32),
-        pltpu.VMEM((nx + 2, nj, S, L), F32),
+        pltpu.VMEM((CYCLES + 1, nx + 2, nj, S, L), F32),
         pltpu.VMEM((2, nx, L), F32),
         pltpu.VMEM((S, L), F32),
+        pltpu.VMEM((S, L), F32),
     ]
 
 
-def shared_scratch(rows):
+def shared_scratch(rows, halves):
     return [
         pltpu.VMEM((2, 2, 2, rows, L), F32),
         pltpu.VMEM((2, 2, 2, rows, L), F32),
@@ -53,6 +59,8 @@
         pltpu.VMEM((CYCLES + 1, 2, S, L), F32),
         pltpu.VMEM((CYCLES + 1, 2, S, L), F32),
         pltpu.VMEM((2, 2, 2, S, L), F32),
+        pltpu.VMEM((2, 2, 3, halves, S, L), F32),
+        pltpu.VMEM((2, 2, 3, halves, S, L), F32),
     ]
 
 
@@ -60,8 +68,8 @@
     fine = Level(0, nx, nj, 1, 0, scratch[0:5])
     coarse = Level(1, nx // 2, nj // 2, 2, nx, scratch[5:10])
     levels = (coarse, fine)
-    YS, YR, ZS, ZR, CS, CR, ZXR, ZYR, YZR, FYS, FYR, FZS, FZR, ZXS = scratch[10:24]
-    PB, PX, PY, PZ, YX, f_ref, d_ref, isem, ssem, rsem = scratch[24:]
+    YS, YR, ZS, ZR, CS, CR, ZXR, ZYR, YZR, FYS, FYR, FZS, FZR, ZXS, XS, XR = scratch[10:26]
+    PB, PX, PY, PZ, YX, f_ref, d_ref, isem, ssem, rsem = scratch[26:]
     loads = [
         pltpu.make_async_copy(f_hbm, f_ref, isem.at[0]),
         pltpu.make_async_copy(d_hbm, d_ref, isem.at[1]),
@@ -107,28 +115,28 @@
             out.append(("edges", ZXS.at[q, u], ZXR.at[q, 1 - u], (dx, 0, 1)))
             for v, dy in enumerate((-1, 1)):
                 out.append(("edges", CS.at[q, u, v], CR.at[q, 1 - u, 1 - v], (dx, dy, 0)))
-        for lv in levels:
-            n = lv.nx
-            k = 1 if lv is fine and stage == STAGES - 1 else 2
-            low, high = (2, k), (2 + n - k, k)
-            to_low, to_high = (2 - k, k), (2 + n, k)
-            if stage == 0:
-                for ref in [lv.F.at[cycle]] + [lv.G] * (cycle == 0):
-                    out.append(("planes", ref.at[1], ref.at[1 + n], (-1, 0, 0)))
-                    out.append(("planes", ref.at[n], ref.at[0], (1, 0, 0)))
-                low, high, to_low, to_high = (3, 1), (n, 1), (0, 1), (3 + n, 1)
-            out.append(("planes", lv.E.at[q, pl.ds(*low)], lv.E.at[q, pl.ds(*to_high)], (-1, 0, 0)))
-            out.append(("planes", lv.E.at[q, pl.ds(*high)], lv.E.at[q, pl.ds(*to_low)], (1, 0, 0)))
+        fields = pl.ds(field_of(cycle), 2 if cycle == 0 else 1)
+        count = 2 if stage or cycle else 3
+        for u, dx in enumerate((-1, 1)):
+            out.append(("planes", XS.at[q, u, pl.ds(0, count)], XR.at[q, 1 - u, pl.ds(0, count)], (dx, 0, 0)))
+        k = 1 if stage == STAGES - 1 else 2
+        low, high = (2, k), (2 + nx - k, k)
+        to_low, to_high = (2 - k, k), (2 + nx, k)
+        if stage == 0:
+            out.append(("planes", fine.FG.at[fields, 1], fine.FG.at[fields, 1 + nx], (-1, 0, 0)))
+            out.append(("planes", fine.FG.at[fields, nx], fine.FG.at[fields, 0], (1, 0, 0)))
+            low, high, to_low, to_high = (3, 1), (nx, 1), (0, 1), (3 + nx, 1)
+        out.append(("planes", fine.E.at[q, pl.ds(*low)], fine.E.at[q, pl.ds(*to_high)], (-1, 0, 0)))
+        out.append(("planes", fine.E.at[q, pl.ds(*high)], fine.E.at[q, pl.ds(*to_low)], (1, 0, 0)))
         out.append(("small", ZS.at[q], ZR.at[q], (0, 0, 1)))
         for v, dy in enumerate((-1, 1)):
             out.append(("small", YS.at[q, v, 0], YZR.at[q, 1 - v], (0, dy, 1)))
             out.append(("small", ZS.at[q, pl.ds(0, 2)], ZYR.at[q, 1 - v], (0, dy, 1)))
             out.append(("small", YS.at[q, v], YR.at[q, 1 - v], (0, dy, 0)))
         if stage == 0:
-            for i in [cycle] + [CYCLES] * (cycle == 0):
-                out.append(("small", FZS.at[i], FZR.at[i], (0, 0, 1)))
-                for v, dy in enumerate((-1, 1)):
-                    out.append(("small", FYS.at[i, v], FYR.at[i, 1 - v], (0, dy, 0)))
+            out.append(("small", FZS.at[fields], FZR.at[fields], (0, 0, 1)))
+            for v, dy in enumerate((-1, 1)):
+                out.append(("small", FYS.at[fields, v], FYR.at[fields, 1 - v], (0, dy, 0)))
         assert len(out) <= COPIES
         return list(enumerate(out))
 
@@ -137,8 +145,8 @@
         return pltpu.make_async_remote_copy(
             src_ref=src,
             dst_ref=dst,
-            send_sem=ssem.at[rnd, i],
-            recv_sem=rsem.at[rnd, i],
+            send_sem=ssem.at[rnd % 2, i],
+            recv_sem=rsem.at[rnd % 2, i],
             device_id=device(d),
             device_id_type=MESH,
         )
@@ -183,7 +191,19 @@
     def packed(lv, acc, depth=0):
         return jnp.where(left, turn(acc, lv.dz * (depth + 1)), turn(acc, -lv.dz * depth))
 
-    def put(lv, slot, q, x, tiles, accs):
+    def squeeze(q, u, slot, tiles):
+        for i in range(0, len(tiles), 2):
+            XS[q, u, slot, i // 2] = jnp.where(even, tiles[i], tiles[i + 1])
+
+    def widen(q, u, slot):
+        out = []
+        for i in range(coarse.nj // 2):
+            t = XR[q, u, slot, i]
+            out.append(jnp.where(even, t, pltpu.roll(t, 1, 1)))
+            out.append(jnp.where(even, pltpu.roll(t, L - 1, 1), t))
+        return out
+
+    def put(lv, slot, q, x, tiles, accs, first=False):
         for j, t in enumerate(tiles):
             lv.E[slot, x + 2, j] = t
             accs = pack(lv, x * lv.nj + j, t, accs)
@@ -191,6 +211,12 @@
         for depth in range(2):
             YS[q, 0, depth, at, :] = tiles[depth][0:1]
             YS[q, 1, depth, at, :] = tiles[-1 - depth][S - 1 : S]
+        if lv is coarse and (x < 2 or x >= lv.nx - 2):
+            depth = x if x < 2 else lv.nx - 1 - x
+            if not first:
+                squeeze(q, 0 if x < 2 else 1, depth, tiles)
+            elif depth == 1:
+                squeeze(q, 0 if x < 2 else 1, 0, tiles)
         if x in (0, lv.nx - 1):
             u = 0 if x == 0 else 1
             for v, t in enumerate((tiles[0][0:1], tiles[-1][S - 1 : S])):
@@ -205,12 +231,14 @@
         for depth, acc in enumerate(accs):
             ZS[q, 2 * depth + lv.at] = packed(lv, acc, depth)
 
-    def put_face(lv, i, x, tiles, acc):
+    def put_face(lv, q, i, x, tiles, acc):
         for j, t in enumerate(tiles):
             (acc,) = pack(lv, x * lv.nj + j, t, [acc])
         at = slice(lv.y0 + x, lv.y0 + x + 1)
         FYS[i, 0, at, :] = tiles[0][0:1]
         FYS[i, 1, at, :] = tiles[-1][S - 1 : S]
+        if lv is coarse and x in (0, lv.nx - 1):
+            squeeze(q, 0 if x == 0 else 1, 2 if i == CYCLES else 1, tiles)
         return acc
 
     def outer(lv):
@@ -240,7 +268,7 @@
 
     def step(lv, cycle, x, c, sums):
         return [
-            (1.0 - W) * c[j] + lv.G[x + 1, j] * (lv.F[cycle, x + 1, j] + sums[j]) for j in range(lv.nj)
+            (1.0 - W) * c[j] + lv.G[x + 1, j] * (lv.F[cycle][x + 1, j] + sums[j]) for j in range(lv.nj)
         ]
 
     def y_rows(lv, ref, x):
@@ -283,7 +311,7 @@
                 zp = turn(jnp.where(lane < lv.dz, jnp.where(left, z, 0.0), c[t]), -lv.dz)
                 zm = turn(jnp.where(lane >= L - lv.dz, jnp.where(left, 0.0, z), c[t]), lv.dz)
                 sums = (xm + xp) + (YR[q, v, 1, a, :] + YS[q, v, 0, a, :]) + (zm + zp)
-                g, f = FYR[CYCLES, v, a, :], FYR[cycle, v, a, :]
+                g, f = FYR[CYCLES, v, a, :], FYR[field_of(cycle), v, a, :]
                 lv.YC[v, pl.ds(S * t, S), :] = (1.0 - W) * c[t] + g * (f + sums)
 
     def z_face(lv, cycle, q):
@@ -298,10 +326,12 @@
         ym = jnp.where(a < dz, pltpu.roll(low, 1, 0), turn(c, dz))
         yp = jnp.where(a >= n - dz, pltpu.roll(high, S - 1, 0), turn(c, -dz))
         sums = (xm + xp) + (ym + yp) + (ZR[q, 2 + lv.at] + ZS[q, lv.at])
-        lv.ZC[...] = (1.0 - W) * c + FZR[CYCLES, lv.at] * (FZR[cycle, lv.at] + sums)
+        new = (1.0 - W) * c + FZR[CYCLES, lv.at] * (FZR[field_of(cycle), lv.at] + sums)
+        lv.ZC[...] = halo_of(lv, new)
+        lv.ZN[...] = new
 
     def second_sweep(lv, cycle, q, xs, accs):
-        halo = halo_of(lv, lv.ZC[...])
+        halo = lv.ZC[...]
         for x in xs:
             rows = [lv.YC[v, x : x + 1, :] for v in range(2)]
             accs = put(lv, q, q, x, own_plane(lv, cycle, 2, x, halo, rows), accs)
@@ -325,16 +355,16 @@
                     g = W / (6.0 + cd)
                     coarse.G[X + 1, J] = g
                 else:
-                    cf = restrict([fine.F[cycle, x + 1, j] for x, j in cells])
+                    cf = restrict([fine.F[cycle][x + 1, j] for x, j in cells])
                     g = coarse.G[X + 1, J]
-                coarse.F[cycle, X + 1, J] = cf
+                coarse.F[cycle][X + 1, J] = cf
                 fs.append(cf)
                 gs.append(g)
                 new.append(g * cf)
-            accs = put(coarse, q, q, X, new, accs)
-            fz = put_face(coarse, cycle, X, fs, fz)
+            accs = put(coarse, q, q, X, new, accs, True)
+            fz = put_face(coarse, q, field_of(cycle), X, fs, fz)
             if first:
-                gz = put_face(coarse, CYCLES, X, gs, gz)
+                gz = put_face(coarse, q, CYCLES, X, gs, gz)
         return accs, fz, gz
 
     def begin_fine(cycle, q, xs, carry):
@@ -347,18 +377,18 @@
                     y = pl.ds(j, S, stride=nj)
                     f = f_ref[x, y, :]
                     g = W / (6.0 + d_ref[x, y, :])
-                    fine.F[cycle, x + 1, j] = f
+                    fine.F[cycle][x + 1, j] = f
                     fine.G[x + 1, j] = g
                 else:
-                    f = fine.F[cycle, x + 1, j]
+                    f = fine.F[cycle][x + 1, j]
                     g = fine.G[x + 1, j]
                 fs.append(f)
                 gs.append(g)
                 new.append(g * f)
-            accs = put(fine, q, q, x, new, accs)
-            fz = put_face(fine, cycle, x, fs, fz)
+            accs = put(fine, q, q, x, new, accs, True)
+            fz = put_face(fine, q, field_of(cycle), x, fs, fz)
             if first:
-                gz = put_face(fine, CYCLES, x, gs, gz)
+                gz = put_face(fine, q, CYCLES, x, gs, gz)
         return accs, fz, gz
 
     def begin(cycle, before=None):
@@ -378,7 +408,7 @@
         high = begin_fine(cycle, q, inner(fine), high)
         for lv, (accs, fz, gz) in ((coarse, low), (fine, high)):
             put_end(lv, q, accs)
-            FZS[cycle, lv.at] = packed(lv, fz)
+            FZS[field_of(cycle), lv.at] = packed(lv, fz)
             if cycle == 0:
                 FZS[CYCLES, lv.at] = packed(lv, gz)
         send(rnd, "small")
@@ -389,9 +419,9 @@
                 lv.E[slot, plane] = jnp.zeros((lv.nj, S, L), F32)
         for plane in (0, lv.nx + 1):
             for cycle in range(CYCLES):
-                lv.F[cycle, plane] = jnp.zeros((lv.nj, S, L), F32)
+                lv.F[cycle][plane] = jnp.zeros((lv.nj, S, L), F32)
             lv.G[plane] = jnp.zeros((lv.nj, S, L), F32)
-    for ref in (YR, CR, CS, ZXR, ZYR, YZR, FYR):
+    for ref in (YR, CR, CS, ZXR, ZYR, YZR, FYR, XR):
         ref[...] = jnp.zeros(ref.shape, F32)
 
     barrier = pltpu.get_barrier_semaphore()
@@ -412,18 +442,33 @@
             swept = levels[: 1 if last else 2]
             wait(rnd, "edges", "small")
             for lv in swept:
+                z_face(lv, cycle, q)
+            for lv in swept:
+                y_faces(lv, cycle, q)
+            for lv in swept:
                 first_sweep(lv, cycle, q, range(1, lv.nx - 1))
-                y_faces(lv, cycle, q)
-                z_face(lv, cycle, q)
             wait(rnd, "planes")
+            for u in range(2):
+                beside, beyond = (1, 0) if u == 0 else (coarse.nx + 2, coarse.nx + 3)
+                for j, t in enumerate(widen(q, u, 0)):
+                    coarse.E[q, beyond if stage == 0 else beside, j] = t
+                for j, t in enumerate(widen(q, u, 1)):
+                    if stage == 0:
+                        coarse.F[cycle][u * (coarse.nx + 1), j] = t
+                    else:
+                        coarse.E[q, beyond, j] = t
+                if stage == 0 and cycle == 0:
+                    for j, t in enumerate(widen(q, u, 2)):
+                        coarse.G[u * (coarse.nx + 1), j] = t
             if stage == 0:
                 for lv in levels:
                     for x in (-1, lv.nx):
                         for j in range(lv.nj):
-                            lv.E[q, x + 2, j] = lv.G[x + 1, j] * lv.F[cycle, x + 1, j]
+                            lv.E[q, x + 2, j] = lv.G[x + 1, j] * lv.F[cycle][x + 1, j]
+            for lv in swept:
+                x_faces(lv, cycle, q)
             for lv in swept:
                 first_sweep(lv, cycle, q, (0, lv.nx - 1))
-                x_faces(lv, cycle, q)
             if not last:
                 accs = [second_sweep(lv, cycle, 1 - q, outer(lv), [zero] * 2) for lv in levels]
                 send(rnd + 1, "edges", "planes")
@@ -432,6 +477,20 @@
                 send(rnd + 1, "small")
                 drain(rnd)
 
+        for v in range(2):
+            for i in range(2):
+                YX[v, pl.ds(i, coarse.nx, stride=2), :] = coarse.YC[v]
+            t = YR[q, v, 0, 0:nx, :] + YX[v]
+            PY[v] = t if cycle == 0 else t + PY[v]
+        z = coarse.ZN[...]
+        t = zero
+        for x in range(nx):
+            here = (lane >= nj * x) & (lane < nj * (x + 1))
+            t = jnp.where(here, turn(z, nj * (x - x // 2)), t)
+        t = t + ZR[q, 0]
+        t = t if cycle == 0 else t + PZ[0]
+        PZ[0] = t
+        PZ[1] = halo_of(fine, t)
         for x in range(-1, nx + 1):
             own = 0 <= x < nx
             for j in range(nj):
@@ -445,28 +504,16 @@
                     PB[x, j] = t
                 else:
                     p_ref[x, pl.ds(j, S, stride=nj), :] = t
-        for v in range(2):
-            for i in range(2):
-                YX[v, pl.ds(i, coarse.nx, stride=2), :] = coarse.YC[v]
-            t = YR[q, v, 0, 0:nx, :] + YX[v]
-            PY[v] = t if cycle == 0 else t + PY[v]
-        z = coarse.ZC[...]
-        t = zero
-        for x in range(nx):
-            here = (lane >= nj * x) & (lane < nj * (x + 1))
-            t = jnp.where(here, turn(z, nj * (x - x // 2)), t)
-        t = t + ZR[q, 0]
-        PZ[...] = t if cycle == 0 else t + PZ[...]
 
         def rest(xs, cycle=cycle):
-            halo = halo_of(fine, PZ[...])
+            halo = PZ[1]
             for x in xs:
                 c, sums = around(fine, 2, x, x * nj, halo, [PY[v, x : x + 1, :] for v in range(2)])
                 for j in range(nj):
                     at = pl.ds(j, S, stride=nj)
                     r = f_ref[x, at, :] - ((6.0 + d_ref[x, at, :]) * c[j] - sums[j])
                     if cycle < CYCLES - 1:
-                        fine.F[cycle + 1, x + 1, j] = r
+                        fine.F[cycle + 1][x + 1, j] = r
                     else:
                         r_ref[x, at, :] = r
 
@@ -484,7 +531,7 @@
     def body(right_side, diagonal):
         nx, ny, nz = right_side.shape
         nj = ny // S
-        assert nz == L and ny % (2 * S) == 0 and nx % (2 * S) == 0 and nx * nj == L and nj & (nj - 1) == 0
+        assert nz == L and ny % (2 * S) == 0 and nx % (2 * S) == 0 and nx * nj == L and nj & (nj - 1) == 0 and nj >= 4
         shape = jax.ShapeDtypeStruct(right_side.shape, F32)
         vmem = pl.BlockSpec(memory_space=pltpu.VMEM)
         hbm = pl.BlockSpec(memory_space=pltpu.HBM)
@@ -495,18 +542,18 @@
             out_specs=(vmem, vmem),
             scratch_shapes=level_scratch(nx, nj)
             + level_scratch(nx // 2, nj // 2)
-            + shared_scratch(nx + nx // 2)
+            + shared_scratch(nx + nx // 2, nj // 4)
             + [
                 pltpu.VMEM((nx, nj, S, L), F32),
                 pltpu.VMEM((2, nj, S, L), F32),
                 pltpu.VMEM((2, nx, L), F32),
-                pltpu.VMEM((S, L), F32),
+                pltpu.VMEM((2, S, L), F32),
                 pltpu.VMEM((2, nx, L), F32),
                 pltpu.VMEM(right_side.shape, F32),
                 pltpu.VMEM(right_side.shape, F32),
                 pltpu.SemaphoreType.DMA((2,)),
-                pltpu.SemaphoreType.DMA((CYCLES * STAGES, COPIES)),
-                pltpu.SemaphoreType.DMA((CYCLES * STAGES, COPIES)),
+                pltpu.SemaphoreType.DMA((2, COPIES)),
+                pltpu.SemaphoreType.DMA((2, COPIES)),
             ],
             compiler_params=pltpu.CompilerParams(
                 collective_id=0, has_side_effects=True, vmem_limit_bytes=32 * 1024 * 1024

time: 46.5 us -> 43.3 us (0.931)
  Pallas kernels: 42 us -> 38.8 us
    pallas_call x1, Pallas kernels: 42 us -> 38.8 us  [body(): pl.pallas_call(functools.partial(kernel, sizes, nx, nj), out_shape=(shape...]
where the time goes in v2:
time: 43.3 us; the launch traced here: 43.1 us
  Pallas kernels  38.8 us (90%)
  local copies, waits for them, and re-layouts  3.66 us (8%)
  between operations  0.65 us (2%)
    pallas_call x1, Pallas kernels, body(): pl.pallas_call(functools.partial(kernel, sizes, nx, nj), out_shape=(shape...  38.8 us
    unnamed x6, local copies, waits for them, and re-layouts  3.66 us

profile of v2, /device:TPU:0, one launch (start us, length us, event | category | flops | bytes accessed | tf_op | source)
XLA Modules:
  0.0 43.1 jit_solution(5089042188160976656)
XLA Ops:
  0.6 0.0 copy-start
  0.6 1.0 %copy-done = f32[16,64,128]{2,1,0:T(8,128)S(1)} copy-done((f32[16,64,128]{2,1,0:T(8,128)S(1)}, f32[16,64,128]{2,1,0:T(8,128)}, u32[]{:S(2)}) %copy-start) | copy-done | bytes 524312
  1.7 0.0 copy-start.1
  1.7 1.0 %copy-done.1 = f32[16,64,128]{2,1,0:T(8,128)S(1)} copy-done((f32[16,64,128]{2,1,0:T(8,128)S(1)}, f32[16,64,128]{2,1,0:T(8,128)}, u32[]{:S(2)}) %copy-start.1) | copy-done | bytes 524312
  2.7 38.8 %shard_map.41 = (f32[16,64,128]{2,1,0:T(8,128)S(1)}, f32[16,64,128]{2,1,0:T(8,128)S(1)}) custom-call(f32[16,64,128]{2,1,0:T(8,128)S(1)} %copy-done, f32[16,64,128]{2,1,0:T(8,128)S(1)} %copy-done.1), custom_call_target="tpu_custom_call" | custom-call | tf_op jit(solution)/shard_map/pallas_call | solution.py:538
  41.5 0.8 %copy.6 = f32[16,64,128]{2,1,0:T(8,128)} copy(f32[16,64,128]{2,1,0:T(8,128)S(1)} %get-tuple-element.4) | data formatting | bytes 1048576
  42.3 0.8 %copy.7 = f32[16,64,128]{2,1,0:T(8,128)} copy(f32[16,64,128]{2,1,0:T(8,128)S(1)} %get-tuple-element.5) | data formatting | bytes 1048576
Async XLA Ops:
  0.6 1.0 %copy-start = (f32[16,64,128]{2,1,0:T(8,128)S(1)}, f32[16,64,128]{2,1,0:T(8,128)}, u32[]{:S(2)}) copy-start(f32[16,64,128]{2,1,0:T(8,128)} %f_hbm.1) | copy-start | bytes 1572868
  1.7 1.0 %copy-start.1 = (f32[16,64,128]{2,1,0:T(8,128)S(1)}, f32[16,64,128]{2,1,0:T(8,128)}, u32[]{:S(2)}) copy-start(f32[16,64,128]{2,1,0:T(8,128)} %d_hbm.1) | copy-start | bytes 1572868

commit v3 on v2

--- a/solution.py
+++ b/solution.py
@@ -119,15 +119,15 @@
         count = 2 if stage or cycle else 3
         for u, dx in enumerate((-1, 1)):
             out.append(("planes", XS.at[q, u, pl.ds(0, count)], XR.at[q, 1 - u, pl.ds(0, count)], (dx, 0, 0)))
-        k = 1 if stage == STAGES - 1 else 2
-        low, high = (2, k), (2 + nx - k, k)
-        to_low, to_high = (2 - k, k), (2 + nx, k)
         if stage == 0:
             out.append(("planes", fine.FG.at[fields, 1], fine.FG.at[fields, 1 + nx], (-1, 0, 0)))
             out.append(("planes", fine.FG.at[fields, nx], fine.FG.at[fields, 0], (1, 0, 0)))
-            low, high, to_low, to_high = (3, 1), (nx, 1), (0, 1), (3 + nx, 1)
-        out.append(("planes", fine.E.at[q, pl.ds(*low)], fine.E.at[q, pl.ds(*to_high)], (-1, 0, 0)))
-        out.append(("planes", fine.E.at[q, pl.ds(*high)], fine.E.at[q, pl.ds(*to_low)], (1, 0, 0)))
+        for depth in range(2):
+            if (stage, depth) in ((0, 0), (STAGES - 1, 1)):
+                continue
+            kind = "beyond" if depth else "planes"
+            out.append((kind, fine.E.at[q, 2 + depth], fine.E.at[q, 2 + nx + depth], (-1, 0, 0)))
+            out.append((kind, fine.E.at[q, 1 + nx - depth], fine.E.at[q, 1 - depth], (1, 0, 0)))
         out.append(("small", ZS.at[q], ZR.at[q], (0, 0, 1)))
         for v, dy in enumerate((-1, 1)):
             out.append(("small", YS.at[q, v, 0], YZR.at[q, 1 - v], (0, dy, 1)))
@@ -171,7 +171,7 @@
         each(rnd, kinds, lambda c: c.wait_recv(), -1)
 
     def drain(rnd):
-        each(rnd, ("edges", "planes", "small"), lambda c: c.wait_send())
+        each(rnd, ("edges", "planes", "small", "beyond"), lambda c: c.wait_send())
 
     def turn(t, by):
         by %= L
@@ -242,10 +242,11 @@
         return acc
 
     def outer(lv):
-        return [0, 1, lv.nx - 2, lv.nx - 1]
+        n = lv.nx
+        return [0, n - 1] if lv is fine else [0, 1, n - 2, n - 1]
 
     def inner(lv):
-        return list(range(2, lv.nx - 2))
+        return [x for x in (1, lv.nx - 2, *range(2, lv.nx - 2)) if x not in outer(lv)]
 
     def halo_of(lv, z):
         return jnp.where(left, turn(z, -lv.dz), z)
@@ -412,6 +413,7 @@
             if cycle == 0:
                 FZS[CYCLES, lv.at] = packed(lv, gz)
         send(rnd, "small")
+        send(rnd, "beyond")
 
     for lv in levels:
         for slot in range(2):
@@ -447,7 +449,7 @@
                 y_faces(lv, cycle, q)
             for lv in swept:
                 first_sweep(lv, cycle, q, range(1, lv.nx - 1))
-            wait(rnd, "planes")
+            wait(rnd, "planes", "beyond")
             for u in range(2):
                 beside, beyond = (1, 0) if u == 0 else (coarse.nx + 2, coarse.nx + 3)
                 for j, t in enumerate(widen(q, u, 0)):
@@ -475,6 +477,7 @@
                 for lv, acc in zip(levels, accs):
                     put_end(lv, 1 - q, second_sweep(lv, cycle, 1 - q, inner(lv), acc))
                 send(rnd + 1, "small")
+                send(rnd + 1, "beyond")
                 drain(rnd)
 
         for v in range(2):

time: 43.3 us -> 42.6 us (0.984)
  Pallas kernels: 38.8 us -> 38 us
    pallas_call x1, Pallas kernels: 38.8 us -> 38 us  [body(): pl.pallas_call(functools.partial(kernel, sizes, nx, nj), out_shape=(shape...]
where the time goes in v3:
time: 42.6 us; the launch traced here: 42.4 us
  Pallas kernels  38 us (89%)
  local copies, waits for them, and re-layouts  3.66 us (9%)
  between operations  0.65 us (2%)
    pallas_call x1, Pallas kernels, body(): pl.pallas_call(functools.partial(kernel, sizes, nx, nj), out_shape=(shape...  38 us
    unnamed x6, local copies, waits for them, and re-layouts  3.66 us

profile of v3, /device:TPU:0, one launch (start us, length us, event | category | flops | bytes accessed | tf_op | source)
XLA Modules:
  0.0 42.4 jit_solution(1237425367266626144)
XLA Ops:
  0.6 0.0 copy-start
  0.6 1.0 %copy-done = f32[16,64,128]{2,1,0:T(8,128)S(1)} copy-done((f32[16,64,128]{2,1,0:T(8,128)S(1)}, f32[16,64,128]{2,1,0:T(8,128)}, u32[]{:S(2)}) %copy-start) | copy-done | bytes 524312
  1.7 0.0 copy-start.1
  1.7 1.0 %copy-done.1 = f32[16,64,128]{2,1,0:T(8,128)S(1)} copy-done((f32[16,64,128]{2,1,0:T(8,128)S(1)}, f32[16,64,128]{2,1,0:T(8,128)}, u32[]{:S(2)}) %copy-start.1) | copy-done | bytes 524312
  2.7 38.0 %shard_map.41 = (f32[16,64,128]{2,1,0:T(8,128)S(1)}, f32[16,64,128]{2,1,0:T(8,128)S(1)}) custom-call(f32[16,64,128]{2,1,0:T(8,128)S(1)} %copy-done, f32[16,64,128]{2,1,0:T(8,128)S(1)} %copy-done.1), custom_call_target="tpu_custom_call" | custom-call | tf_op jit(solution)/shard_map/pallas_call | solution.py:541
  40.8 0.8 %copy.6 = f32[16,64,128]{2,1,0:T(8,128)} copy(f32[16,64,128]{2,1,0:T(8,128)S(1)} %get-tuple-element.4) | data formatting | bytes 1048576
  41.6 0.8 %copy.7 = f32[16,64,128]{2,1,0:T(8,128)} copy(f32[16,64,128]{2,1,0:T(8,128)S(1)} %get-tuple-element.5) | data formatting | bytes 1048576
Async XLA Ops:
  0.6 1.0 %copy-start = (f32[16,64,128]{2,1,0:T(8,128)S(1)}, f32[16,64,128]{2,1,0:T(8,128)}, u32[]{:S(2)}) copy-start(f32[16,64,128]{2,1,0:T(8,128)} %f_hbm.1) | copy-start | bytes 1572868
  1.7 1.0 %copy-start.1 = (f32[16,64,128]{2,1,0:T(8,128)S(1)}, f32[16,64,128]{2,1,0:T(8,128)}, u32[]{:S(2)}) copy-start(f32[16,64,128]{2,1,0:T(8,128)} %d_hbm.1) | copy-start | bytes 1572868
